TPU v7x, 256 devices: a whole 4x4x8 slice. The times are simulated.
256 devices in a mesh: row: 8 (over x_lo, y), col: 32 (over x_hi, z, core).
Axes of the slice: x: 4 (x_hi: 2, x_lo: 2; x = x_hi * 2 + x_lo), y: 4, z: 8, core: 2. Of those that a mesh axis runs over, the one named last changes fastest.
Arguments:
- images: bfloat16 [2, 256, 512, 512], P(None, 'row', 'col'), may hold values from -6 to 6
- labels: int32 [256, 512], P('row', 'col'), may hold values from 0 to 2
- qkv_weight: bfloat16 [512, 1536], replicated, may hold values from -0.25 to 0.25
- proj_weight: bfloat16 [512, 512], replicated, may hold values from -0.25 to 0.25
- up_weight: bfloat16 [512, 2048], replicated, may hold values from -0.25 to 0.25
- down_weight: bfloat16 [2048, 512], replicated, may hold values from -0.125 to 0.125
- head_scale: float32 [16], replicated, may hold values from 3 to 12
- cross_qkv: bfloat16 [512, 1536], replicated, may hold values from -0.25 to 0.25
- cross_proj: bfloat16 [512, 512], replicated, may hold values from -0.25 to 0.25
- cross_scale: float32 [16], replicated, may hold values from 3 to 12
- diff_up: bfloat16 [512, 1024], replicated, may hold values from -0.25 to 0.25
- diff_down: bfloat16 [1024, 512], replicated, may hold values from -0.1875 to 0.1875
Outputs:
- change: bfloat16 [256, 512, 512], P('row', 'col')
All inputs are finite; a program needn't handle non-finite values.
Results may differ from a plain program's by a relative error of at most 0.015.
Values may be sent and summed in bfloat16 or wider, within the bound.
A program may use at most 192 MiB of HBM per device.

v0:
```python
import functools
import math

import jax
import jax.numpy as jnp
from jax import lax
from jax.experimental import pallas as pl
from jax.experimental.pallas import tpu as pltpu
from jax.sharding import PartitionSpec as P

WIN = 8
SHIFT = 4
HEADS = 16
C = 512
CELL = SHIFT * SHIFT
EPS = 1e-5
LOG2E = math.log2(math.e)
BF = jnp.bfloat16
F32 = jnp.float32
MESH = pl.DeviceIdType.MESH


def dot(a, b):
    return jnp.dot(a, b, preferred_element_type=F32)


def dot_t(a, b):
    return lax.dot_general(a, b, (((1,), (1,)), ((), ())), preferred_element_type=F32)


def iota(shape, dim):
    return lax.broadcasted_iota(jnp.int32, shape, dim)


def norm_rows(v):
    mean = jnp.sum(v, axis=-1, keepdims=True) * (1.0 / C)
    centre = v - mean
    spread = jnp.sum(centre * centre, axis=-1, keepdims=True) * (1.0 / C)
    return centre * lax.rsqrt(spread + EPS)


def gelu_twice(v):
    k = math.sqrt(2.0 / math.pi)
    inner = v * (k + (k * 0.044715) * (v * v))
    return v * (1.0 + jnp.tanh(inner))


def kernel(
    rows, cols, remote,
    img, lab, hs, cs, wqkv_h, wp_h, wu_h, wd_h, cqkv_h, cp_h, du_h, dd_h,
    out,
    im, wqkv, wp, wu, wd, cqkv, cp, du, dd,
    xc, gc, sc, perm, bd, ones4, scale_s, xs, qkv_s, att_s, hid_s, first_s, ob,
    im_sem, w_sem, out_sem, send1, recv1, send2, recv2,
):
    me_r = lax.axis_index("row") if remote else 0
    me_c = lax.axis_index("col") if remote else 0
    up, down = lax.rem(me_r + rows - 1, rows), lax.rem(me_r + 1, rows)
    left, right = lax.rem(me_c + cols - 1, cols), lax.rem(me_c + 1, cols)

    weights = [
        (wqkv_h, wqkv), (wp_h, wp), (wu_h, wu), (wd_h, wd),
        (cqkv_h, cqkv), (cp_h, cp), (du_h, du), (dd_h, dd),
    ]
    loads = [pltpu.make_async_copy(s, d, w_sem.at[n]) for n, (s, d) in enumerate(weights)]
    load_im = pltpu.make_async_copy(img, im, im_sem)
    load_im.start()
    for load in loads:
        load.start()

    if remote:
        barrier = pltpu.get_barrier_semaphore()
        for r, c in ((up, me_c), (down, me_c), (me_r, left), (me_r, right), (up, left), (down, right)):
            pl.semaphore_signal(barrier, inc=1, device_id={"row": r, "col": c}, device_id_type=MESH)

    o = iota((256, 256), 0)
    t = iota((256, 256), 1)
    src = ((o // 64) * 4 + (o // 4) % 4) * 16 + ((o // 16) % 4) * 4 + o % 4
    perm[...] = jnp.where(src == t, 1.0, 0.0).astype(BF)
    bd[...] = jnp.where(o // 32 == t // 32, 1.0, 0.0).astype(BF)
    o4 = iota((512, 128), 0)
    t4 = iota((512, 128), 1)
    ones4[0] = jnp.where((o4 % 256) // 64 == t4 // 32, 1.0, 0.0).astype(BF)
    ones4[1] = jnp.where(o4 // 128 == t4 // 32, 1.0, 0.0).astype(BF)
    lane = iota((8, C), 1) // 32
    for n, ref in ((0, hs), (1, cs)):
        row = jnp.zeros((8, C), F32)
        for h in range(HEADS):
            row = jnp.where(lane == h, ref[h] * LOG2E, row)
        scale_s[n] = row

    tok = iota((512, 32), 0)
    tr = (tok // 64) * 4 + (tok // 4) % 4
    pick_r = jnp.where(tr == iota((512, 32), 1), 1.0, 0.0).astype(BF)
    tok = iota((512, 16), 0)
    tc = ((tok // 16) % 4) * 4 + tok % 4
    by_row = dot(pick_r, lab[...].astype(F32).astype(BF))
    picked = jnp.where(tc == iota((512, 16), 1), by_row, 0.0).astype(BF)
    value = dot(picked, jnp.ones((16, 128), BF)).astype(jnp.int32)
    tok = iota((512, 128), 0)
    gr = (tok // 64) * 4 + (tok // 4) % 4 + me_r * 32
    gcol = ((tok // 16) % 4) * 4 + tok % 4 + me_c * 16
    code = value * 4 + jnp.where(gr < SHIFT, 2, 0) + jnp.where(gcol < SHIFT, 1, 0)
    onehot = jnp.where(code == iota((512, 128), 1), 1.0, 0.0).astype(BF)
    gc[0:8, 0:4] = onehot.reshape(8, 4, CELL, 128)

    load_im.wait()
    for d in range(2):
        for b in range(2):
            block = im[d, 16 * b : 16 * b + 16].reshape(256, C)
            cells = dot(perm[...], block).astype(BF)
            xc[d, 4 * b : 4 * b + 4, 0:4] = cells.reshape(4, 4, CELL, C)

    def send(src, dst, n, r, c, sems, rsems):
        return pltpu.make_async_remote_copy(
            src_ref=src, dst_ref=dst, send_sem=sems.at[n], recv_sem=rsems.at[n],
            device_id={"row": r, "col": c}, device_id_type=MESH,
        )

    if remote:
        pl.semaphore_wait(barrier, 6)
        halo = [
            send(xc.at[:, 1:8, 0], xc.at[:, 1:8, 4], 0, me_r, left, send1, recv1),
            send(gc.at[1:8, 0], gc.at[1:8, 4], 1, me_r, left, send1, recv1),
            send(xc.at[:, 0, 1:4], xc.at[:, 8, 1:4], 2, up, me_c, send1, recv1),
            send(gc.at[0, 1:4], gc.at[8, 1:4], 3, up, me_c, send1, recv1),
            send(xc.at[:, 0, 0], xc.at[:, 8, 4], 4, up, left, send1, recv1),
            send(gc.at[0, 0], gc.at[8, 4], 5, up, left, send1, recv1),
        ]
        for copy in halo:
            copy.start()
        back = [
            send(sc.at[:, 1:7, 4], sc.at[:, 1:7, 0], 0, me_r, right, send2, recv2),
            send(sc.at[:, 7, 4], sc.at[:, 7, 0], 1, me_r, right, send2, recv2),
            send(sc.at[:, 8, 1:4], sc.at[:, 0, 1:4], 2, down, me_c, send2, recv2),
            send(sc.at[:, 8, 4], sc.at[:, 0, 0], 3, down, right, send2, recv2),
        ]

    head_of = iota((1, 128), 1) // 32
    head_mask = [jnp.where(head_of == h, 1.0, 0.0).astype(BF) for h in range(4)]

    def packed_qkv(x, w, scale):
        for n in range(6):
            y = dot(x, w[:, 256 * n : 256 * n + 256]).astype(BF)
            if n < 4:
                ss = dot(y * y, bd[...])
                factor = lax.rsqrt(jnp.maximum(ss, 1.0))
                if n < 2:
                    factor = factor * scale[:, 256 * n : 256 * n + 256]
                y = (y.astype(F32) * factor).astype(BF)
            qkv_s[:, 256 * n : 256 * n + 256] = y

    def stacked(v):
        return jnp.concatenate([v * head_mask[h] for h in range(4)], 0)

    def attend(base, count, ones, mask):
        for g in range(4):
            lanes = slice(128 * g, 128 * g + 128)
            q = qkv_s[base : base + count, lanes]
            k = qkv_s[base : base + count, 512 + 128 * g : 640 + 128 * g]
            v = qkv_s[base : base + count, 1024 + 128 * g : 1152 + 128 * g]
            e = jnp.exp2(dot_t(q, stacked(k))).astype(BF)
            if mask is not None:
                e = e * mask
            o = dot(e, jnp.concatenate([stacked(v), ones], 1))
            att_s[base : base + count, lanes] = (o[:, :128] / o[:, 128:]).astype(BF)

    for n in range(4):
        loads[n].wait()

    def block_step(step, carry):
        if remote:
            @pl.when(step == 1)
            def _():
                halo[0].wait_recv()
                halo[1].wait_recv()

            @pl.when(step == 3)
            def _():
                for copy in halo[2:]:
                    copy.wait_recv()

        spots = []
        for n in range(2):
            p = 2 * step + n
            a = jnp.where(p < 6, lax.rem(p, 3), 3)
            b = jnp.where(p < 6, p // 3, p - 6)
            spots.append((2 * a + 1, 2 * b + 1))
        for n, (i, j) in enumerate(spots):
            for d in range(2):
                for u in range(2):
                    for v in range(2):
                        at = 128 * n + 64 * d + 32 * u + 16 * v
                        xs[at : at + 16] = xc[d, i + u, j + v]
        x = xs[...]
        packed_qkv(x, wqkv, scale_s[0, 0:1])
        for n, (i, j) in enumerate(spots):
            g = jnp.concatenate([gc[i + u, j + v] for u in range(2) for v in range(2)], 0)
            mask = dot_t(g, jnp.concatenate([g] * 4, 0)).astype(BF)
            for d in range(2):
                attend(128 * n + 64 * d, 64, ones4[0, 0:256], mask)
        first = (x.astype(F32) + norm_rows(dot(att_s[...], wp[...]))).astype(BF)
        first_s[...] = first
        for n in range(8):
            h = dot(first, wu[:, 256 * n : 256 * n + 256])
            hid_s[:, 256 * n : 256 * n + 256] = gelu_twice(h).astype(BF)
        second = (first_s[...].astype(F32) + norm_rows(0.5 * dot(hid_s[...], wd[...]))).astype(BF)
        for n, (i, j) in enumerate(spots):
            for d in range(2):
                for u in range(2):
                    for v in range(2):
                        at = 128 * n + 64 * d + 32 * u + 16 * v
                        sc[d, i + u, j + v] = second[at : at + 16]
        if remote:
            @pl.when(step == 2)
            def _():
                back[0].start()

            @pl.when(step == 3)
            def _():
                for copy in back[1:]:
                    copy.start()
        return carry

    lax.fori_loop(0, 4, block_step, 0)
    for n in range(4, 8):
        loads[n].wait()

    def cross_step(step, carry):
        band = lax.rem(step + 1, 4)
        if remote:
            @pl.when(step == 0)
            def _():
                back[0].wait_recv()

            @pl.when(step == 2)
            def _():
                back[1].wait_recv()

            @pl.when(step == 3)
            def _():
                back[2].wait_recv()
                back[3].wait_recv()

        for n in range(2):
            for d in range(2):
                for u in range(2):
                    for v in range(2):
                        at = 128 * n + 64 * d + 32 * u + 16 * v
                        xs[at : at + 16] = sc[d, 2 * band + u, 2 * n + v]
        x = xs[...]
        packed_qkv(x, cqkv, scale_s[1, 0:1])
        for n in range(2):
            attend(128 * n, 128, ones4[1], None)
        joined = x.astype(F32) + norm_rows(dot(att_s[...], cp[...]))
        contrast = jnp.concatenate(
            [joined[64:128] - joined[0:64], joined[192:256] - joined[128:192]], 0
        )
        operand = contrast.astype(BF)
        for n in range(4):
            h = dot(operand, du[:, 256 * n : 256 * n + 256])
            hid_s[0:128, 256 * n : 256 * n + 256] = gelu_twice(h).astype(BF)
        change = (contrast + norm_rows(0.5 * dot(hid_s[0:128, 0:1024], dd[...]))).astype(BF)
        oo = iota((128, 128), 0)
        tt = iota((128, 128), 1)
        r, c = oo // 16, oo % 16
        spot = (c // 8) * 64 + (r // 4) * 32 + ((c // 4) % 2) * 16 + (r % 4) * 4 + c % 4
        order = jnp.where(spot == tt, 1.0, 0.0).astype(BF)
        ob[band] = dot(order, change).astype(BF).reshape(8, 16, C)
        pltpu.make_async_copy(ob.at[band], out.at[pl.ds(8 * band, 8)], out_sem.at[band]).start()
        return carry

    lax.fori_loop(0, 4, cross_step, 0)
    for n in range(4):
        pltpu.make_async_copy(ob.at[n], out.at[pl.ds(8 * n, 8)], out_sem.at[n]).wait()
    if remote:
        for copy in halo + back:
            copy.wait_send()


def device_program(rows, cols, remote, images, labels, qkv_weight, proj_weight, up_weight, down_weight,
                   head_scale, cross_qkv, cross_proj, cross_scale, diff_up, diff_down):
    any_spec = pl.BlockSpec(memory_space=pl.ANY)
    vmem = pl.BlockSpec(memory_space=pltpu.VMEM)
    smem = pl.BlockSpec(memory_space=pltpu.SMEM)
    big = [qkv_weight, proj_weight, up_weight, down_weight, cross_qkv, cross_proj, diff_up, diff_down]
    dma = pltpu.SemaphoreType.DMA
    return pl.pallas_call(
        functools.partial(kernel, rows, cols, remote),
        out_shape=jax.ShapeDtypeStruct((32, 16, C), BF),
        in_specs=[any_spec, vmem, smem, smem] + [any_spec] * 8,
        out_specs=any_spec,
        scratch_shapes=[
            pltpu.VMEM((2, 32, 16, C), BF),
            *[pltpu.VMEM(w.shape, BF) for w in big],
            pltpu.VMEM((2, 9, 5, CELL, C), BF),
            pltpu.VMEM((9, 5, CELL, 128), BF),
            pltpu.VMEM((2, 9, 5, CELL, C), BF),
            pltpu.VMEM((256, 256), BF),
            pltpu.VMEM((256, 256), BF),
            pltpu.VMEM((2, 512, 128), BF),
            pltpu.VMEM((2, 8, C), F32),
            pltpu.VMEM((256, C), BF),
            pltpu.VMEM((256, 3 * C), BF),
            pltpu.VMEM((256, C), BF),
            pltpu.VMEM((256, 2048), BF),
            pltpu.VMEM((256, C), BF),
            pltpu.VMEM((4, 8, 16, C), BF),
            dma, dma((8,)), dma((4,)), dma((6,)), dma((6,)), dma((4,)), dma((4,)),
        ],
        compiler_params=pltpu.CompilerParams(
            collective_id=0 if remote else None,
            has_side_effects=remote,
            vmem_limit_bytes=56 * 1024 * 1024,
        ),
        cost_estimate=pl.CostEstimate(flops=11_000_000_000, bytes_accessed=13_000_000, transcendentals=6_000_000),
        name="window_pair",
    )(images, labels, head_scale, cross_scale, *big)


def solution(mesh):
    placed = (P(None, "row", "col", None), P("row", "col")) + (P(),) * 10
    body = functools.partial(device_program, mesh.shape["row"], mesh.shape["col"], True)
    return jax.shard_map(
        body, mesh=mesh, in_specs=placed, out_specs=P("row", "col", None), check_vma=False
    )
```

profile of v0, /device:TPU:6, one launch (start us, length us, event | category | flops | bytes accessed | tf_op | source)
XLA Modules:
  0.0 47.0 jit_solution(9009227146530778546)
XLA Ops:
  0.0 1.4 %copy.13.lab = s32[32,16]{1,0:T(8,128)} copy(s32[32,16]{0,1:T(8,128)} %param.13) | data formatting | bytes 4096 | tf_op args[1]
  1.4 43.8 %window_pair.1 = bf16[32,16,512]{2,1,0:T(8,128)(2,1)} custom-call(bf16[2,32,16,512]{3,2,1,0:T(8,128)(2,1)} %img.1, s32[32,16]{1,0:T(8,128)} %copy.13.lab, f32[16]{0:T(128)} %hs.1, f32[16]{0:T(128)} %cs.1, bf16[512,1536]{1,0:T(8,128)(2,1)} %wqkv_h.1, bf16[512,512]{1,0:T(8,128)(2,1)} %wp_h.1, bf16[512,2048]{1,0:T(8,128)(2,1)} %wu_h.1, bf16[2048,512]{1,0:T(8,128)(2,1)} %wd_h.1, ...), custom_call_target="tpu_custom_call" | custom-call | flops 11000000512 | bytes 13000000 | tf_op jit(solution)/shard_map/window_pair/pallas_call | solution.py:288
  45.1 1.9 %copy.15 = bf16[32,16,512]{2,1,0:T(8,128)(2,1)} copy(bf16[32,16,512]{2,1,0:T(8,128)(2,1)} %window_pair.1) | data formatting | bytes 1048576
where the time goes:
time: 47.9 us; the launch traced here: 47 us
  Pallas kernels  43.8 us (91%)
  local copies, waits for them, and re-layouts  3.24 us (7%)
    pallas_call x1, Pallas kernels, device_program(): pl.pallas_call(functools.partial(kernel, rows, cols, remote), out_shape=j...  43.8 us
    unnamed x2, local copies, waits for them, and re-layouts  3.24 us

commit v1 on v0

v1 whole, which is shorter than its diff:
```python
import functools
import math

import jax
import jax.numpy as jnp
from jax import lax
from jax.experimental import pallas as pl
from jax.experimental.pallas import tpu as pltpu
from jax.sharding import PartitionSpec as P

WIN = 8
SHIFT = 4
HEADS = 16
C = 512
CELL = SHIFT * SHIFT
EPS = 1e-5
LOG2E = math.log2(math.e)
BF = jnp.bfloat16
F32 = jnp.float32
MESH = pl.DeviceIdType.MESH


def dot(a, b):
    return jnp.dot(a, b, preferred_element_type=F32)


def dot_t(a, b):
    return lax.dot_general(a, b, (((1,), (1,)), ((), ())), preferred_element_type=F32)


def iota(shape, dim):
    return lax.broadcasted_iota(jnp.int32, shape, dim)


def norm_rows(v):
    mean = jnp.sum(v, axis=-1, keepdims=True) * (1.0 / C)
    centre = v - mean
    spread = jnp.sum(centre * centre, axis=-1, keepdims=True) * (1.0 / C)
    return centre * lax.rsqrt(spread + EPS)


def pieces(count, step=64):
    return [slice(at, min(at + step, count)) for at in range(0, count, step)]


def gelu_twice(v):
    k = math.sqrt(2.0 / math.pi)
    inner = v * (k + (k * 0.044715) * (v * v))
    return v * (1.0 + jnp.tanh(inner))


NEAR = [(0, 0), (1, 0), (2, 0)]
FAR = [(0, 1), (1, 1), (2, 1), (3, 0), (3, 1)]
CROSS_NEAR = [(1, 1), (2, 1), (3, 1)]
CROSS_FAR = [(1, 0), (2, 0), (3, 0), (0, 0), (0, 1)]


def kernel(
    rows, cols, remote,
    img, lab_h, hs, cs, wqkv_h, wp_h, wu_h, wd_h, cqkv_h, cp_h, du_h, dd_h,
    out,
    im, lab, wqkv, wp, wu, wd, cqkv, cp, du, dd,
    xc, gc, sc, perm, bd, ones4, scale_s, qkv_s, att_s, hid_s, first_s, ct_s, ob,
    im_sem, lab_sem, w_sem, out_sem, send1, recv1, send2, recv2,
):
    me_r = lax.axis_index("row") if remote else 0
    me_c = lax.axis_index("col") if remote else 0
    up, down = lax.rem(me_r + rows - 1, rows), lax.rem(me_r + 1, rows)
    left, right = lax.rem(me_c + cols - 1, cols), lax.rem(me_c + 1, cols)

    weights = [
        (wqkv_h, wqkv), (wp_h, wp), (wu_h, wu), (wd_h, wd),
        (cqkv_h, cqkv), (cp_h, cp), (du_h, du), (dd_h, dd),
    ]
    loads = [pltpu.make_async_copy(s, d, w_sem.at[n]) for n, (s, d) in enumerate(weights)]
    load_im = pltpu.make_async_copy(img, im, im_sem)
    load_im.start()
    load_lab = pltpu.make_async_copy(lab_h, lab, lab_sem)
    load_lab.start()
    for load in loads:
        load.start()

    if remote:
        barrier = pltpu.get_barrier_semaphore()
        for r, c in ((up, me_c), (down, me_c), (me_r, left), (me_r, right), (up, left), (down, right)):
            pl.semaphore_signal(barrier, inc=1, device_id={"row": r, "col": c}, device_id_type=MESH)

    o = iota((256, 256), 0)
    t = iota((256, 256), 1)
    src = ((o // 64) * 4 + (o // 4) % 4) * 16 + ((o // 16) % 4) * 4 + o % 4
    perm[...] = jnp.where(src == t, 1.0, 0.0).astype(BF)

    load_im.wait()
    for d in range(2):
        for b in range(2):
            block = im[d, 16 * b : 16 * b + 16].reshape(256, C)
            cells = dot(perm[...], block).astype(BF)
            xc[d, 4 * b : 4 * b + 4, 0:4] = cells.reshape(4, 4, CELL, C)

    def send(src, dst, n, r, c, sems, rsems):
        return pltpu.make_async_remote_copy(
            src_ref=src, dst_ref=dst, send_sem=sems.at[n], recv_sem=rsems.at[n],
            device_id={"row": r, "col": c}, device_id_type=MESH,
        )

    if remote:
        pl.semaphore_wait(barrier, 6)
        halo = [
            send(xc.at[:, 1:8, 0], xc.at[:, 1:8, 4], 0, me_r, left, send1, recv1),
            send(xc.at[:, 0, 1:4], xc.at[:, 8, 1:4], 1, up, me_c, send1, recv1),
            send(xc.at[:, 0, 0], xc.at[:, 8, 4], 2, up, left, send1, recv1),
        ]
        for copy in halo:
            copy.start()

    bd[...] = jnp.where(o // 32 == t // 32, 1.0, 0.0).astype(BF)
    o4 = iota((512, 128), 0)
    t4 = iota((512, 128), 1)
    ones4[0] = jnp.where((o4 % 256) // 64 == t4 // 32, 1.0, 0.0).astype(BF)
    ones4[1] = jnp.where(o4 // 128 == t4 // 32, 1.0, 0.0).astype(BF)
    lane = iota((8, C), 1) // 32
    for n, ref in ((0, hs), (1, cs)):
        row = jnp.zeros((8, C), F32)
        for h in range(HEADS):
            row = jnp.where(lane == h, ref[h] * LOG2E, row)
        scale_s[n] = row

    load_lab.wait()
    tok = iota((512, 16), 0)
    tc = ((tok // 16) % 4) * 4 + tok % 4
    pick_c = jnp.where(tc == iota((512, 16), 1), 1.0, 0.0).astype(BF)
    tok = iota((512, 32), 0)
    tr = (tok // 64) * 4 + (tok // 4) % 4
    by_col = dot(pick_c, lab[...].astype(F32).astype(BF))
    picked = jnp.where(tr == iota((512, 32), 1), by_col, 0.0).astype(BF)
    value = dot(picked, jnp.ones((32, 128), BF)).astype(jnp.int32)
    tok = iota((512, 128), 0)
    gr = (tok // 64) * 4 + (tok // 4) % 4 + me_r * 32
    gcol = ((tok // 16) % 4) * 4 + tok % 4 + me_c * 16
    code = value * 4 + jnp.where(gr < SHIFT, 2, 0) + jnp.where(gcol < SHIFT, 1, 0)
    onehot = jnp.where(code == iota((512, 128), 1), 1.0, 0.0).astype(BF)
    gc[0:8, 0:4] = onehot.reshape(8, 4, CELL, 128)
    if remote:
        codes = [
            send(gc.at[1:8, 0], gc.at[1:8, 4], 3, me_r, left, send1, recv1),
            send(gc.at[0, 1:4], gc.at[8, 1:4], 4, up, me_c, send1, recv1),
            send(gc.at[0, 0], gc.at[8, 4], 5, up, left, send1, recv1),
        ]
        for copy in codes:
            copy.start()
        halo = halo + codes
        back = [
            send(sc.at[:, 1:8, 4], sc.at[:, 1:8, 0], 0, me_r, right, send2, recv2),
            send(sc.at[:, 8, 1:4], sc.at[:, 0, 1:4], 1, down, me_c, send2, recv2),
            send(sc.at[:, 8, 4], sc.at[:, 0, 0], 2, down, right, send2, recv2),
        ]

    head_of = iota((1, 128), 1) // 32
    head_mask = [jnp.where(head_of == h, 1.0, 0.0).astype(BF) for h in range(4)]

    def stacked(v):
        return jnp.concatenate([v * head_mask[h] for h in range(4)], 0)

    def packed_qkv(chains, w, scale):
        for n in range(6):
            lanes = slice(256 * n, 256 * n + 256)
            for base, count, x in chains:
                qkv_s[base : base + count, lanes] = dot(x(), w[:, lanes]).astype(BF)
        for n in range(4):
            lanes = slice(256 * n, 256 * n + 256)
            for base, count, x in chains:
                y = qkv_s[base : base + count, lanes]
                factor = lax.rsqrt(jnp.maximum(dot(y * y, bd[...]), 1.0))
                if n < 2:
                    factor = factor * scale[:, lanes]
                qkv_s[base : base + count, lanes] = (y.astype(F32) * factor).astype(BF)

    def attend(base, count, g, ones, mask):
        lanes = slice(128 * g, 128 * g + 128)
        q = qkv_s[base : base + count, lanes]
        k = qkv_s[base : base + count, 512 + 128 * g : 640 + 128 * g]
        v = qkv_s[base : base + count, 1024 + 128 * g : 1152 + 128 * g]
        e = jnp.exp2(dot_t(q, stacked(k))).astype(BF)
        if mask is not None:
            e = e * mask
        o = dot(e, jnp.concatenate([stacked(v), ones], 1))
        att_s[base : base + count, lanes] = (o[:, :128] * pltpu.reciprocal(o[:, 128:], approx=True)).astype(BF)

    def cells_of(ref, d, spots):
        return jnp.concatenate(
            [ref[d, i + u, j + v] for i, j in spots for u in range(2) for v in range(2)], 0
        )

    def block(windows, waits):
        spots = [(2 * a + 1, 2 * b + 1) for a, b in windows]
        count = 64 * len(spots)
        chains = [(d * count, count, functools.partial(cells_of, xc, d, spots)) for d in range(2)]
        if waits:
            loads[0].wait()
        packed_qkv(chains, wqkv, scale_s[0, 0:1])
        masks = []
        for i, j in spots:
            g = jnp.concatenate([gc[i + u, j + v] for u in range(2) for v in range(2)], 0)
            masks.append(dot_t(g, jnp.concatenate([g] * 4, 0)).astype(BF))
        for n in range(len(spots)):
            for g in range(4):
                for d in range(2):
                    attend(d * count + 64 * n, 64, g, ones4[0, 0:256], masks[n])
        if waits:
            loads[1].wait()
        for base, count, x in chains:
            v = dot(att_s[base : base + count], wp[...])
            res = x()
            for p in pieces(count):
                first = res[p].astype(F32) + norm_rows(v[p])
                first_s[base + p.start : base + p.stop] = first.astype(BF)
        if waits:
            loads[2].wait()
        for n in range(8):
            lanes = slice(256 * n, 256 * n + 256)
            for base, count, x in chains:
                h = dot(first_s[base : base + count], wu[:, lanes])
                hid_s[base : base + count, lanes] = gelu_twice(h).astype(BF)
        if waits:
            loads[3].wait()
        for d, (base, count, x) in enumerate(chains):
            v = dot(hid_s[base : base + count], wd[...])
            for n, (i, j) in enumerate(spots):
                p = slice(64 * n, 64 * n + 64)
                first = first_s[base + p.start : base + p.stop]
                second = (first.astype(F32) + norm_rows(0.5 * v[p])).astype(BF)
                for u in range(2):
                    for v2 in range(2):
                        at = 32 * u + 16 * v2
                        sc[d, i + u, j + v2] = second[at : at + 16]

    def cross(windows):
        chains = []
        for n, (a, b) in enumerate(windows):
            def x(a=a, b=b):
                return jnp.concatenate([cells_of(sc, d, [(2 * a, 2 * b)]) for d in range(2)], 0)
            chains.append((128 * n, 128, x))
        packed_qkv(chains, cqkv, scale_s[1, 0:1])
        for base, count, x in chains:
            for g in range(4):
                attend(base, count, g, ones4[1], None)
        for (base, count, x), (a, b) in zip(chains, windows):
            v = dot(att_s[base : base + count], cp[...])
            res = x()
            past = res[0:64].astype(F32) + norm_rows(v[0:64])
            ct_s[a, 64 * b : 64 * b + 64] = res[64:128].astype(F32) + norm_rows(v[64:128]) - past

    block(NEAR, True)
    if remote:
        for copy in halo:
            copy.wait_recv()
    block(FAR, False)
    if remote:
        for copy in back:
            copy.start()
    for n in range(4, 6):
        loads[n].wait()
    cross(CROSS_NEAR)
    if remote:
        for copy in back:
            copy.wait_recv()
    cross(CROSS_FAR)
    for n in range(6, 8):
        loads[n].wait()

    oo = iota((128, 128), 0)
    tt = iota((128, 128), 1)
    r, c = oo // 16, oo % 16
    spot = (c // 8) * 64 + (r // 4) * 32 + ((c // 4) % 2) * 16 + (r % 4) * 4 + c % 4
    order = jnp.where(spot == tt, 1.0, 0.0).astype(BF)
    halves = (0, 2)
    for n in range(4):
        lanes = slice(256 * n, 256 * n + 256)
        for b in halves:
            operand = ct_s[b : b + 2].reshape(256, C).astype(BF)
            hid_s[128 * b : 128 * b + 256, lanes] = gelu_twice(dot(operand, du[:, lanes])).astype(BF)
    stores = []
    for b in halves:
        v = dot(hid_s[128 * b : 128 * b + 256, 0:1024], dd[...])
        for n in range(2):
            change = jnp.concatenate(
                [
                    (ct_s[b + n, p] + norm_rows(0.5 * v[128 * n + p.start : 128 * n + p.stop])).astype(BF)
                    for p in pieces(128)
                ], 0,
            )
            ob[8 * (b + n) : 8 * (b + n) + 8] = dot(order, change).astype(BF).reshape(8, 16, C)
        store = pltpu.make_async_copy(
            ob.at[pl.ds(8 * b, 16)], out.at[pl.ds(8 * b, 16)], out_sem.at[b // 2]
        )
        store.start()
        stores.append(store)
    for store in stores:
        store.wait()
    if remote:
        for copy in halo + back:
            copy.wait_send()


def device_program(rows, cols, remote, images, labels, qkv_weight, proj_weight, up_weight, down_weight,
                   head_scale, cross_qkv, cross_proj, cross_scale, diff_up, diff_down):
    any_spec = pl.BlockSpec(memory_space=pl.ANY)
    smem = pl.BlockSpec(memory_space=pltpu.SMEM)
    big = [qkv_weight, proj_weight, up_weight, down_weight, cross_qkv, cross_proj, diff_up, diff_down]
    dma = pltpu.SemaphoreType.DMA
    return pl.pallas_call(
        functools.partial(kernel, rows, cols, remote),
        out_shape=jax.ShapeDtypeStruct((32, 16, C), BF),
        in_specs=[any_spec, any_spec, smem, smem] + [any_spec] * 8,
        out_specs=any_spec,
        scratch_shapes=[
            pltpu.VMEM((2, 32, 16, C), BF),
            pltpu.VMEM((16, 32), jnp.int32),
            *[pltpu.VMEM(w.shape, BF) for w in big],
            pltpu.VMEM((2, 9, 5, CELL, C), BF),
            pltpu.VMEM((9, 5, CELL, 128), BF),
            pltpu.VMEM((2, 9, 5, CELL, C), BF),
            pltpu.VMEM((256, 256), BF),
            pltpu.VMEM((256, 256), BF),
            pltpu.VMEM((2, 512, 128), BF),
            pltpu.VMEM((2, 8, C), F32),
            pltpu.VMEM((640, 3 * C), BF),
            pltpu.VMEM((640, C), BF),
            pltpu.VMEM((640, 2048), BF),
            pltpu.VMEM((640, C), BF),
            pltpu.VMEM((4, 128, C), F32),
            pltpu.VMEM((32, 16, C), BF),
            dma, dma, dma((8,)), dma((2,)), dma((6,)), dma((6,)), dma((3,)), dma((3,)),
        ],
        compiler_params=pltpu.CompilerParams(
            collective_id=0 if remote else None,
            has_side_effects=remote,
            vmem_limit_bytes=56 * 1024 * 1024,
        ),
        cost_estimate=pl.CostEstimate(flops=11_000_000_000, bytes_accessed=13_000_000, transcendentals=6_000_000),
        name="window_pair",
    )(images, labels.T, head_scale, cross_scale, *big)


def solution(mesh):
    placed = (P(None, "row", "col", None), P("row", "col")) + (P(),) * 10
    body = functools.partial(device_program, mesh.shape["row"], mesh.shape["col"], True)
    return jax.shard_map(
        body, mesh=mesh, in_specs=placed, out_specs=P("row", "col", None), check_vma=False
    )
```

time: 47.9 us -> 40.9 us (0.85)
  Pallas kernels: 43.8 us -> 38.2 us
  local copies, waits for them, and re-layouts: 3.24 us -> 1.87 us
    pallas_call x1, Pallas kernels: 43.8 us -> 38.2 us  [device_program(): pl.pallas_call(functools.partial(kernel, rows, cols, remote), out_shape=j...]
    unnamed x2 -> x1, local copies, waits for them, and re-layouts: 3.24 us -> 1.87 us
where the time goes in v1:
time: 40.9 us; the launch traced here: 40 us
  Pallas kernels  38.2 us (93%)
  local copies, waits for them, and re-layouts  1.87 us (5%)
    pallas_call x1, Pallas kernels, device_program(): pl.pallas_call(functools.partial(kernel, rows, cols, remote), out_shape=j...  38.2 us
    unnamed x1, local copies, waits for them, and re-layouts  1.87 us

profile of v1, /device:TPU:6, one launch (start us, length us, event | category | flops | bytes accessed | tf_op | source)
XLA Modules:
  0.0 40.0 jit_solution(12944664250889656746)
XLA Ops:
  0.0 38.2 %window_pair.1 = bf16[32,16,512]{2,1,0:T(8,128)(2,1)} custom-call(bf16[2,32,16,512]{3,2,1,0:T(8,128)(2,1)} %img.1, s32[16,32]{1,0:T(8,128)} %bitcast.1, f32[16]{0:T(128)} %hs.1, f32[16]{0:T(128)} %cs.1, bf16[512,1536]{1,0:T(8,128)(2,1)} %wqkv_h.1, bf16[512,512]{1,0:T(8,128)(2,1)} %wp_h.1, bf16[512,2048]{1,0:T(8,128)(2,1)} %wu_h.1, bf16[2048,512]{1,0:T(8,128)(2,1)} %wd_h.1, ...), custom_call_target="tpu_custom_call" | custom-call | flops 11000000512 | bytes 13000000 | tf_op jit(solution)/shard_map/window_pair/pallas_call | solution.py:311
  38.2 1.9 %copy.14 = bf16[32,16,512]{2,1,0:T(8,128)(2,1)} copy(bf16[32,16,512]{2,1,0:T(8,128)(2,1)} %window_pair.1) | data formatting | bytes 1048576

commit v2 on v1

v2 whole, which is shorter than its diff:
```python
import functools
import math

import jax
import jax.numpy as jnp
from jax import lax
from jax.experimental import pallas as pl
from jax.experimental.pallas import tpu as pltpu
from jax.sharding import PartitionSpec as P

WIN = 8
SHIFT = 4
HEADS = 16
C = 512
CELL = SHIFT * SHIFT
EPS = 1e-5
LOG2E = math.log2(math.e)
BF = jnp.bfloat16
F32 = jnp.float32
MESH = pl.DeviceIdType.MESH


def dot(a, b):
    return jnp.dot(a, b, preferred_element_type=F32)


def dot_t(a, b):
    return lax.dot_general(a, b, (((1,), (1,)), ((), ())), preferred_element_type=F32)


def iota(shape, dim):
    return lax.broadcasted_iota(jnp.int32, shape, dim)


def norm_rows(v):
    mean = jnp.sum(v, axis=-1, keepdims=True) * (1.0 / C)
    centre = v - mean
    spread = jnp.sum(centre * centre, axis=-1, keepdims=True) * (1.0 / C)
    return centre * lax.rsqrt(spread + EPS)


def pieces(count, step=64):
    return [slice(at, min(at + step, count)) for at in range(0, count, step)]


def gelu_twice(v):
    k = math.sqrt(2.0 / math.pi)
    inner = v * (k + (k * 0.044715) * (v * v))
    return v * (1.0 + jnp.tanh(inner))


BLOCK = [(d, a, 0) for d in range(2) for a in range(3)]
BLOCK += [(d, a, b) for d in range(2) for a, b in ((0, 1), (1, 1), (2, 1), (3, 0), (3, 1))]
BLOCK_NEAR, BLOCK_FAR = (0, 3, 6), (6, 11, 16)
CROSS = [(1, 1), (2, 1), (3, 1), (1, 0), (2, 0), (3, 0), (0, 0), (0, 1)]
CROSS_NEAR, CROSS_FAR = range(3), range(3, 8)


def cell_rows():
    block, cross = [], []
    for n, (d, a, b) in enumerate(BLOCK):
        for u in range(2):
            for v in range(2):
                block.append(((d, 2 * a + 1 + u, 2 * b + 1 + v), 64 * n + 32 * u + 16 * v))
    for n, (a, b) in enumerate(CROSS):
        for d in range(2):
            for u in range(2):
                for v in range(2):
                    cross.append(((d, 2 * a + u, 2 * b + v), 128 * n + 64 * d + 32 * u + 16 * v))
    return block, cross


def kernel(
    rows, cols, remote,
    img, lab_h, hs, cs, wqkv_h, wp_h, wu_h, wd_h, cqkv_h, cp_h, du_h, dd_h,
    out,
    im, lab, wqkv, wp, wu, wd, cqkv, cp, du, dd,
    xc, gc, sc, perm, bd, ones4, scale_s, qkv_s, att_s, hid_s, first_s, ct_s, ob,
    im_sem, lab_sem, w_sem, out_sem, send1, recv1, send2, recv2,
):
    me_r = lax.axis_index("row") if remote else 0
    me_c = lax.axis_index("col") if remote else 0
    up, down = lax.rem(me_r + rows - 1, rows), lax.rem(me_r + 1, rows)
    left, right = lax.rem(me_c + cols - 1, cols), lax.rem(me_c + 1, cols)

    weights = [
        (wqkv_h, wqkv), (wp_h, wp), (wu_h, wu), (wd_h, wd),
        (cqkv_h, cqkv), (cp_h, cp), (du_h, du), (dd_h, dd),
    ]
    loads = [pltpu.make_async_copy(s, d, w_sem.at[n]) for n, (s, d) in enumerate(weights)]
    load_im = pltpu.make_async_copy(img, im, im_sem)
    load_im.start()
    load_lab = pltpu.make_async_copy(lab_h, lab, lab_sem)
    load_lab.start()
    loads[0].start()

    if remote:
        barrier = pltpu.get_barrier_semaphore()
        for r, c in ((up, me_c), (down, me_c), (me_r, left), (me_r, right), (up, left), (down, right)):
            pl.semaphore_signal(barrier, inc=1, device_id={"row": r, "col": c}, device_id_type=MESH)

    o = iota((256, 256), 0)
    t = iota((256, 256), 1)
    src = (((o >> 6) * 4 + ((o >> 2) & 3)) * 16) + ((o >> 4) & 3) * 4 + (o & 3)
    perm[...] = jnp.where(src == t, 1.0, 0.0).astype(BF)

    load_im.wait()
    for load in loads[1:4]:
        load.start()
    for d in range(2):
        for b in range(2):
            block = im[d, 16 * b : 16 * b + 16].reshape(256, C)
            cells = dot(perm[...], block).astype(BF)
            xc[d, 4 * b : 4 * b + 4, 0:4] = cells.reshape(4, 4, CELL, C)

    def send(src, dst, n, r, c, sems, rsems):
        return pltpu.make_async_remote_copy(
            src_ref=src, dst_ref=dst, send_sem=sems.at[n], recv_sem=rsems.at[n],
            device_id={"row": r, "col": c}, device_id_type=MESH,
        )

    block_cells, cross_cells = cell_rows()

    def project(ref, cells, w):
        for n in range(6):
            lanes = slice(256 * n, 256 * n + 256)
            for part in cells:
                y = dot(jnp.concatenate([ref[spot] for spot, _ in part], 0), w[:, lanes]).astype(BF)
                for m, (_, row) in enumerate(part):
                    qkv_s[row : row + 16, lanes] = y[16 * m : 16 * m + 16]

    def unit(cells, scale):
        for n in range(4):
            lanes = slice(256 * n, 256 * n + 256)
            for part in cells:
                y = jnp.concatenate([qkv_s[row : row + 16, lanes] for _, row in part], 0)
                factor = lax.rsqrt(jnp.maximum(dot(y * y, bd[...]), 1.0))
                if n < 2:
                    factor = factor * scale[:, lanes]
                y = (y.astype(F32) * factor).astype(BF)
                for m, (_, row) in enumerate(part):
                    qkv_s[row : row + 16, lanes] = y[16 * m : 16 * m + 16]

    def by_date(cells, here):
        return [[c for c in cells if c[0][0] == d and here(c[0]) ] for d in range(2)]

    own_block = by_date(block_cells, lambda c: c[1] < 8 and c[2] < 4)
    far_block = by_date(block_cells, lambda c: not (c[1] < 8 and c[2] < 4))
    own_cross = by_date(cross_cells, lambda c: c[1] > 0 and c[2] > 0)
    far_cross = by_date(cross_cells, lambda c: not (c[1] > 0 and c[2] > 0))

    loads[0].wait()
    project(xc, own_block, wqkv)
    for load in loads[4:]:
        load.start()

    if remote:
        pl.semaphore_wait(barrier, 6)
        halo = [
            send(xc.at[:, 1:8, 0], xc.at[:, 1:8, 4], 0, me_r, left, send1, recv1),
            send(xc.at[:, 0, 1:4], xc.at[:, 8, 1:4], 1, up, me_c, send1, recv1),
            send(xc.at[:, 0, 0], xc.at[:, 8, 4], 2, up, left, send1, recv1),
        ]
        for copy in halo:
            copy.start()

    bd[...] = jnp.where((o >> 5) == (t >> 5), 1.0, 0.0).astype(BF)
    o4 = iota((512, 128), 0)
    t4 = iota((512, 128), 1)
    ones4[0] = jnp.where(((o4 >> 6) & 3) == (t4 >> 5), 1.0, 0.0).astype(BF)
    ones4[1] = jnp.where((o4 >> 7) == (t4 >> 5), 1.0, 0.0).astype(BF)
    lane = iota((8, C), 1) >> 5
    for n, ref in ((0, hs), (1, cs)):
        row = jnp.zeros((8, C), F32)
        for h in range(HEADS):
            row = jnp.where(lane == h, ref[h] * LOG2E, row)
        scale_s[n] = row

    unit(own_block, scale_s[0, 0:1])

    load_lab.wait()
    tok = iota((512, 16), 0)
    tc = ((tok >> 4) & 3) * 4 + (tok & 3)
    pick_c = jnp.where(tc == iota((512, 16), 1), 1.0, 0.0).astype(BF)
    tok = iota((512, 32), 0)
    tr = (tok >> 6) * 4 + ((tok >> 2) & 3)
    by_col = dot(pick_c, lab[...].astype(F32).astype(BF))
    picked = jnp.where(tr == iota((512, 32), 1), by_col, 0.0).astype(BF)
    value = dot(picked, jnp.ones((32, 128), BF)).astype(jnp.int32)
    tok = iota((512, 128), 0)
    gr = (tok >> 6) * 4 + ((tok >> 2) & 3) + me_r * 32
    gcol = ((tok >> 4) & 3) * 4 + (tok & 3) + me_c * 16
    code = value * 4 + jnp.where(gr < SHIFT, 2, 0) + jnp.where(gcol < SHIFT, 1, 0)
    onehot = jnp.where(code == iota((512, 128), 1), 1.0, 0.0).astype(BF)
    gc[0:8, 0:4] = onehot.reshape(8, 4, CELL, 128)
    if remote:
        codes = [
            send(gc.at[1:8, 0], gc.at[1:8, 4], 3, me_r, left, send1, recv1),
            send(gc.at[0, 1:4], gc.at[8, 1:4], 4, up, me_c, send1, recv1),
            send(gc.at[0, 0], gc.at[8, 4], 5, up, left, send1, recv1),
        ]
        for copy in codes:
            copy.start()
        halo = halo + codes
        back = [
            send(sc.at[:, 1:8, 4], sc.at[:, 1:8, 0], 0, me_r, right, send2, recv2),
            send(sc.at[:, 8, 1:4], sc.at[:, 0, 1:4], 1, down, me_c, send2, recv2),
            send(sc.at[:, 8, 4], sc.at[:, 0, 0], 2, down, right, send2, recv2),
        ]

    head_of = iota((1, 128), 1) >> 5
    head_mask = [jnp.where(head_of == h, 1.0, 0.0).astype(BF) for h in range(4)]

    def stacked(v):
        return jnp.concatenate([v * head_mask[h] for h in range(4)], 0)

    def attend(base, count, g, ones, mask):
        lanes = slice(128 * g, 128 * g + 128)
        q = qkv_s[base : base + count, lanes]
        k = qkv_s[base : base + count, 512 + 128 * g : 640 + 128 * g]
        v = qkv_s[base : base + count, 1024 + 128 * g : 1152 + 128 * g]
        e = jnp.exp2(dot_t(q, stacked(k))).astype(BF)
        if mask is not None:
            e = e * mask
        o = dot(e, jnp.concatenate([stacked(v), ones], 1))
        att_s[base : base + count, lanes] = (o[:, :128] * pltpu.reciprocal(o[:, 128:], approx=True)).astype(BF)

    def cells_of(ref, d, i, j):
        return [ref[d, i + u, j + v] for u in range(2) for v in range(2)]

    def spot_of(n):
        d, a, b = BLOCK[n]
        return d, 2 * a + 1, 2 * b + 1

    def block(first_n, mid_n, last_n, waits):
        chains = [(64 * lo, 64 * hi) for lo, hi in ((first_n, mid_n), (mid_n, last_n))]
        for n in range(first_n, mid_n):
            _, i, j = spot_of(n)
            g = jnp.concatenate([gc[i + u, j + v] for u in range(2) for v in range(2)], 0)
            mask = dot_t(g, jnp.concatenate([g] * 4, 0)).astype(BF)
            for g in range(4):
                for m in (n, n + mid_n - first_n):
                    attend(64 * m, 64, g, ones4[0, 0:256], mask)
        if waits:
            loads[1].wait()
        for lo, hi in chains:
            v = dot(att_s[lo:hi], wp[...])
            for row in range(lo, hi, 64):
                res = jnp.concatenate(cells_of(xc, *spot_of(row // 64)), 0)
                first = res.astype(F32) + norm_rows(v[row - lo : row - lo + 64])
                first_s[row : row + 64] = first.astype(BF)
        if waits:
            loads[2].wait()
        for n in range(8):
            lanes = slice(256 * n, 256 * n + 256)
            for lo, hi in chains:
                hid_s[lo:hi, lanes] = gelu_twice(dot(first_s[lo:hi], wu[:, lanes])).astype(BF)
        if waits:
            loads[3].wait()
        for lo, hi in chains:
            v = dot(hid_s[lo:hi], wd[...])
            for row in range(lo, hi, 64):
                d, i, j = spot_of(row // 64)
                first = first_s[row : row + 64].astype(F32)
                second = (first + norm_rows(0.5 * v[row - lo : row - lo + 64])).astype(BF)
                for u in range(2):
                    for v2 in range(2):
                        at = 32 * u + 16 * v2
                        sc[d, i + u, j + v2] = second[at : at + 16]

    def cross(windows):
        for n in windows:
            for g in range(4):
                attend(128 * n, 128, g, ones4[1], None)
        for n in windows:
            a, b = CROSS[n]
            v = dot(att_s[128 * n : 128 * n + 128], cp[...])
            res = [jnp.concatenate(cells_of(sc, d, 2 * a, 2 * b), 0).astype(F32) for d in range(2)]
            past = res[0] + norm_rows(v[0:64])
            ct_s[a, 64 * b : 64 * b + 64] = res[1] + norm_rows(v[64:128]) - past

    block(*BLOCK_NEAR, True)
    if remote:
        for copy in halo:
            copy.wait_recv()
    project(xc, far_block, wqkv)
    unit(far_block, scale_s[0, 0:1])
    block(*BLOCK_FAR, False)
    if remote:
        for copy in back:
            copy.start()
    for n in range(4, 6):
        loads[n].wait()
    project(sc, own_cross, cqkv)
    unit(own_cross, scale_s[1, 0:1])
    cross(CROSS_NEAR)
    if remote:
        for copy in back:
            copy.wait_recv()
    project(sc, far_cross, cqkv)
    unit(far_cross, scale_s[1, 0:1])
    cross(CROSS_FAR)
    for n in range(6, 8):
        loads[n].wait()

    oo = iota((128, 128), 0)
    tt = iota((128, 128), 1)
    r, c = oo >> 4, oo & 15
    spot = (c >> 3) * 64 + (r >> 2) * 32 + ((c >> 2) & 1) * 16 + (r & 3) * 4 + (c & 3)
    order = jnp.where(spot == tt, 1.0, 0.0).astype(BF)
    halves = (0, 2)
    for n in range(4):
        lanes = slice(256 * n, 256 * n + 256)
        for b in halves:
            operand = ct_s[b : b + 2].reshape(256, C).astype(BF)
            hid_s[128 * b : 128 * b + 256, lanes] = gelu_twice(dot(operand, du[:, lanes])).astype(BF)
    for b in halves:
        v = dot(hid_s[128 * b : 128 * b + 256, 0:1024], dd[...])
        for n in range(2):
            change = jnp.concatenate(
                [
                    (ct_s[b + n, p] + norm_rows(0.5 * v[128 * n + p.start : 128 * n + p.stop])).astype(BF)
                    for p in pieces(128)
                ], 0,
            )
            out[8 * (b + n) : 8 * (b + n) + 8] = dot(order, change).astype(BF).reshape(8, 16, C)
    if remote:
        for copy in halo + back:
            copy.wait_send()


def device_program(rows, cols, remote, images, labels, qkv_weight, proj_weight, up_weight, down_weight,
                   head_scale, cross_qkv, cross_proj, cross_scale, diff_up, diff_down):
    any_spec = pl.BlockSpec(memory_space=pl.ANY)
    smem = pl.BlockSpec(memory_space=pltpu.SMEM)
    big = [qkv_weight, proj_weight, up_weight, down_weight, cross_qkv, cross_proj, diff_up, diff_down]
    dma = pltpu.SemaphoreType.DMA
    return pl.pallas_call(
        functools.partial(kernel, rows, cols, remote),
        out_shape=pltpu.VMEM((32, 16, C), BF),
        in_specs=[any_spec, any_spec, smem, smem] + [any_spec] * 8,
        out_specs=pl.BlockSpec(memory_space=pltpu.VMEM),
        scratch_shapes=[
            pltpu.VMEM((2, 32, 16, C), BF),
            pltpu.VMEM((16, 32), jnp.int32),
            *[pltpu.VMEM(w.shape, BF) for w in big],
            pltpu.VMEM((2, 9, 5, CELL, C), BF),
            pltpu.VMEM((9, 5, CELL, 128), BF),
            pltpu.VMEM((2, 9, 5, CELL, C), BF),
            pltpu.VMEM((256, 256), BF),
            pltpu.VMEM((256, 256), BF),
            pltpu.VMEM((2, 512, 128), BF),
            pltpu.VMEM((2, 8, C), F32),
            pltpu.VMEM((1024, 3 * C), BF),
            pltpu.VMEM((1024, C), BF),
            pltpu.VMEM((1024, 2048), BF),
            pltpu.VMEM((1024, C), BF),
            pltpu.VMEM((4, 128, C), F32),
            pltpu.VMEM((32, 16, C), BF),
            dma, dma, dma((8,)), dma((2,)), dma((6,)), dma((6,)), dma((3,)), dma((3,)),
        ],
        compiler_params=pltpu.CompilerParams(
            collective_id=0 if remote else None,
            has_side_effects=remote,
            vmem_limit_bytes=60 * 1024 * 1024,
        ),
        cost_estimate=pl.CostEstimate(flops=11_000_000_000, bytes_accessed=13_000_000, transcendentals=6_000_000),
        name="window_pair",
    )(images, labels.T, head_scale, cross_scale, *big)


def solution(mesh):
    placed = (P(None, "row", "col", None), P("row", "col")) + (P(),) * 10
    body = functools.partial(device_program, mesh.shape["row"], mesh.shape["col"], True)
    return jax.shard_map(
        body, mesh=mesh, in_specs=placed, out_specs=P("row", "col", None), check_vma=False
    )
```

time: 40.9 us -> 38.1 us (0.932)
  Pallas kernels: 38.2 us -> 36.8 us
  local copies, waits for them, and re-layouts: 1.87 us -> 0.8 us
    pallas_call x1, Pallas kernels: 38.2 us -> 36.8 us  [device_program(): pl.pallas_call(functools.partial(kernel, rows, cols, remote), out_shape=p...]
    unnamed x1, local copies, waits for them, and re-layouts: 1.87 us -> 0.8 us
where the time goes in v2:
time: 38.1 us; the launch traced here: 37.6 us
  Pallas kernels  36.8 us (97%)
  local copies, waits for them, and re-layouts  0.8 us (2%)
    pallas_call x1, Pallas kernels, device_program(): pl.pallas_call(functools.partial(kernel, rows, cols, remote), out_shape=p...  36.8 us
    unnamed x1, local copies, waits for them, and re-layouts  0.8 us

profile of v2, /device:TPU:6, one launch (start us, length us, event | category | flops | bytes accessed | tf_op | source)
XLA Modules:
  0.0 37.6 jit_solution(16321922803085692198)
XLA Ops:
  0.0 36.8 %window_pair.1 = bf16[32,16,512]{2,1,0:T(8,128)(2,1)S(1)} custom-call(bf16[2,32,16,512]{3,2,1,0:T(8,128)(2,1)} %img.1, s32[16,32]{1,0:T(8,128)} %bitcast.1, f32[16]{0:T(128)} %hs.1, f32[16]{0:T(128)} %cs.1, bf16[512,1536]{1,0:T(8,128)(2,1)} %wqkv_h.1, bf16[512,512]{1,0:T(8,128)(2,1)} %wp_h.1, bf16[512,2048]{1,0:T(8,128)(2,1)} %wu_h.1, ...), custom_call_target="tpu_custom_call" | custom-call | flops 11000000512 | bytes 13000000 | tf_op jit(solution)/shard_map/window_pair/pallas_call | solution.py:338
  36.8 0.8 %copy.14 = bf16[32,16,512]{2,1,0:T(8,128)(2,1)} copy(bf16[32,16,512]{2,1,0:T(8,128)(2,1)S(1)} %window_pair.1) | data formatting | bytes 1048576

commit v3 on v2

--- a/solution.py
+++ b/solution.py
@@ -83,6 +83,8 @@
     up, down = lax.rem(me_r + rows - 1, rows), lax.rem(me_r + 1, rows)
     left, right = lax.rem(me_c + cols - 1, cols), lax.rem(me_c + 1, cols)
 
+    early = lax.rem(me_c, cols // 2) == 0
+
     weights = [
         (wqkv_h, wqkv), (wp_h, wp), (wu_h, wu), (wd_h, wd),
         (cqkv_h, cqkv), (cp_h, cp), (du_h, du), (dd_h, dd),
@@ -149,20 +151,29 @@
     own_cross = by_date(cross_cells, lambda c: c[1] > 0 and c[2] > 0)
     far_cross = by_date(cross_cells, lambda c: not (c[1] > 0 and c[2] > 0))
 
+    def on(condition):
+        return pl.when(condition) if remote else (lambda work: work())
+
+    if remote:
+        halo = [
+            send(xc.at[:, 1:8, 0], xc.at[:, 1:8, 4], 0, me_r, left, send1, recv1),
+            send(xc.at[:, 0, 1:4], xc.at[:, 8, 1:4], 1, up, me_c, send1, recv1),
+            send(xc.at[:, 0, 0], xc.at[:, 8, 4], 2, up, left, send1, recv1),
+            send(gc.at[1:8, 0], gc.at[1:8, 4], 3, me_r, left, send1, recv1),
+            send(gc.at[0, 1:4], gc.at[8, 1:4], 4, up, me_c, send1, recv1),
+            send(gc.at[0, 0], gc.at[8, 4], 5, up, left, send1, recv1),
+        ]
+
+        @pl.when(jnp.logical_not(early))
+        def _():
+            pl.semaphore_wait(barrier, 6)
+            for copy in halo[:3]:
+                copy.start()
+
     loads[0].wait()
     project(xc, own_block, wqkv)
     for load in loads[4:]:
         load.start()
-
-    if remote:
-        pl.semaphore_wait(barrier, 6)
-        halo = [
-            send(xc.at[:, 1:8, 0], xc.at[:, 1:8, 4], 0, me_r, left, send1, recv1),
-            send(xc.at[:, 0, 1:4], xc.at[:, 8, 1:4], 1, up, me_c, send1, recv1),
-            send(xc.at[:, 0, 0], xc.at[:, 8, 4], 2, up, left, send1, recv1),
-        ]
-        for copy in halo:
-            copy.start()
 
     bd[...] = jnp.where((o >> 5) == (t >> 5), 1.0, 0.0).astype(BF)
     o4 = iota((512, 128), 0)
@@ -194,14 +205,11 @@
     onehot = jnp.where(code == iota((512, 128), 1), 1.0, 0.0).astype(BF)
     gc[0:8, 0:4] = onehot.reshape(8, 4, CELL, 128)
     if remote:
-        codes = [
-            send(gc.at[1:8, 0], gc.at[1:8, 4], 3, me_r, left, send1, recv1),
-            send(gc.at[0, 1:4], gc.at[8, 1:4], 4, up, me_c, send1, recv1),
-            send(gc.at[0, 0], gc.at[8, 4], 5, up, left, send1, recv1),
-        ]
-        for copy in codes:
-            copy.start()
-        halo = halo + codes
+        @pl.when(jnp.logical_not(early))
+        def _():
+            for copy in halo[3:]:
+                copy.start()
+
         back = [
             send(sc.at[:, 1:8, 4], sc.at[:, 1:8, 0], 0, me_r, right, send2, recv2),
             send(sc.at[:, 8, 1:4], sc.at[:, 0, 1:4], 1, down, me_c, send2, recv2),
@@ -279,16 +287,33 @@
             past = res[0] + norm_rows(v[0:64])
             ct_s[a, 64 * b : 64 * b + 64] = res[1] + norm_rows(v[64:128]) - past
 
-    block(*BLOCK_NEAR, True)
-    if remote:
+    if remote:
+        @pl.when(early)
+        def _():
+            block(*BLOCK_NEAR, True)
+            pl.semaphore_wait(barrier, 6)
+            for copy in halo:
+                copy.start()
+
         for copy in halo:
             copy.wait_recv()
     project(xc, far_block, wqkv)
     unit(far_block, scale_s[0, 0:1])
+
+    @on(jnp.logical_not(early))
+    def _():
+        for n in range(1, 4):
+            loads[n].wait()
+
     block(*BLOCK_FAR, False)
     if remote:
         for copy in back:
             copy.start()
+
+    @on(jnp.logical_not(early))
+    def _():
+        block(*BLOCK_NEAR, False)
+
     for n in range(4, 6):
         loads[n].wait()
     project(sc, own_cross, cqkv)

time: 38.1 us -> 38.7 us (1.016); the launches traced: 37.6 us -> 38.6 us
  Pallas kernels: 36.8 us -> 37.8 us
    pallas_call x1, Pallas kernels: 36.8 us -> 37.8 us  [device_program(): pl.pallas_call(functools.partial(kernel, rows, cols, remote), out_shape=p...]
where the time goes in v3:
time: 38.7 us; the launch traced here: 38.6 us
  Pallas kernels  37.8 us (98%)
  local copies, waits for them, and re-layouts  0.8 us (2%)
    pallas_call x1, Pallas kernels, device_program(): pl.pallas_call(functools.partial(kernel, rows, cols, remote), out_shape=p...  37.8 us
    unnamed x1, local copies, waits for them, and re-layouts  0.8 us

profile of v3, /device:TPU:6, one launch (start us, length us, event | category | flops | bytes accessed | tf_op | source)
XLA Modules:
  0.0 38.6 jit_solution(16688627572450515854)
XLA Ops:
  0.0 37.8 %window_pair.1 = bf16[32,16,512]{2,1,0:T(8,128)(2,1)S(1)} custom-call(bf16[2,32,16,512]{3,2,1,0:T(8,128)(2,1)} %img.1, s32[16,32]{1,0:T(8,128)} %bitcast.1, f32[16]{0:T(128)} %hs.1, f32[16]{0:T(128)} %cs.1, bf16[512,1536]{1,0:T(8,128)(2,1)} %wqkv_h.1, bf16[512,512]{1,0:T(8,128)(2,1)} %wp_h.1, bf16[512,2048]{1,0:T(8,128)(2,1)} %wu_h.1, ...), custom_call_target="tpu_custom_call" | custom-call | flops 11000000512 | bytes 13000000 | tf_op jit(solution)/shard_map/window_pair/pallas_call | solution.py:363
  37.8 0.8 %copy.14 = bf16[32,16,512]{2,1,0:T(8,128)(2,1)} copy(bf16[32,16,512]{2,1,0:T(8,128)(2,1)S(1)} %window_pair.1) | data formatting | bytes 1048576

commit v4 on v3

--- a/solution.py
+++ b/solution.py
@@ -50,8 +50,9 @@
 
 
 BLOCK = [(d, a, 0) for d in range(2) for a in range(3)]
-BLOCK += [(d, a, b) for d in range(2) for a, b in ((0, 1), (1, 1), (2, 1), (3, 0), (3, 1))]
-BLOCK_NEAR, BLOCK_FAR = (0, 3, 6), (6, 11, 16)
+BLOCK += [(d, a, 1) for d in range(2) for a in range(3)]
+BLOCK += [(d, 3, b) for d in range(2) for b in range(2)]
+NEAR, RIGHT, BELOW = (0, 3, 6), (6, 9, 12), (12, 14, 16)
 CROSS = [(1, 1), (2, 1), (3, 1), (1, 0), (2, 0), (3, 0), (0, 0), (0, 1)]
 CROSS_NEAR, CROSS_FAR = range(3), range(3, 8)
 
@@ -75,8 +76,8 @@
     img, lab_h, hs, cs, wqkv_h, wp_h, wu_h, wd_h, cqkv_h, cp_h, du_h, dd_h,
     out,
     im, lab, wqkv, wp, wu, wd, cqkv, cp, du, dd,
-    xc, gc, sc, perm, bd, ones4, scale_s, qkv_s, att_s, hid_s, first_s, ct_s, ob,
-    im_sem, lab_sem, w_sem, out_sem, send1, recv1, send2, recv2,
+    xc, gc, sc, perm, bd, ones4, scale_s, qkv_s, att_s, hid_s, first_s, ct_s, ch_s,
+    im_sem, lab_sem, w_sem, send1, recv1, send2, recv2,
 ):
     me_r = lax.axis_index("row") if remote else 0
     me_c = lax.axis_index("col") if remote else 0
@@ -147,7 +148,8 @@
         return [[c for c in cells if c[0][0] == d and here(c[0]) ] for d in range(2)]
 
     own_block = by_date(block_cells, lambda c: c[1] < 8 and c[2] < 4)
-    far_block = by_date(block_cells, lambda c: not (c[1] < 8 and c[2] < 4))
+    right_block = [[c for c in block_cells if c[0][1] < 7 and c[0][2] == 4]]
+    below_block = [[c for c in block_cells if c[0][1] == 8 or c[0][1:] == (7, 4)]]
     own_cross = by_date(cross_cells, lambda c: c[1] > 0 and c[2] > 0)
     far_cross = by_date(cross_cells, lambda c: not (c[1] > 0 and c[2] > 0))
 
@@ -156,18 +158,19 @@
 
     if remote:
         halo = [
-            send(xc.at[:, 1:8, 0], xc.at[:, 1:8, 4], 0, me_r, left, send1, recv1),
+            send(xc.at[:, 1:7, 0], xc.at[:, 1:7, 4], 0, me_r, left, send1, recv1),
             send(xc.at[:, 0, 1:4], xc.at[:, 8, 1:4], 1, up, me_c, send1, recv1),
-            send(xc.at[:, 0, 0], xc.at[:, 8, 4], 2, up, left, send1, recv1),
-            send(gc.at[1:8, 0], gc.at[1:8, 4], 3, me_r, left, send1, recv1),
-            send(gc.at[0, 1:4], gc.at[8, 1:4], 4, up, me_c, send1, recv1),
-            send(gc.at[0, 0], gc.at[8, 4], 5, up, left, send1, recv1),
+            send(xc.at[:, 7, 0], xc.at[:, 7, 4], 2, me_r, left, send1, recv1),
+            send(xc.at[:, 0, 0], xc.at[:, 8, 4], 3, up, left, send1, recv1),
+            send(gc.at[1:8, 0], gc.at[1:8, 4], 4, me_r, left, send1, recv1),
+            send(gc.at[0, 1:4], gc.at[8, 1:4], 5, up, me_c, send1, recv1),
+            send(gc.at[0, 0], gc.at[8, 4], 6, up, left, send1, recv1),
         ]
 
         @pl.when(jnp.logical_not(early))
         def _():
             pl.semaphore_wait(barrier, 6)
-            for copy in halo[:3]:
+            for copy in halo[:4]:
                 copy.start()
 
     loads[0].wait()
@@ -207,13 +210,14 @@
     if remote:
         @pl.when(jnp.logical_not(early))
         def _():
-            for copy in halo[3:]:
+            for copy in halo[4:]:
                 copy.start()
 
         back = [
-            send(sc.at[:, 1:8, 4], sc.at[:, 1:8, 0], 0, me_r, right, send2, recv2),
-            send(sc.at[:, 8, 1:4], sc.at[:, 0, 1:4], 1, down, me_c, send2, recv2),
-            send(sc.at[:, 8, 4], sc.at[:, 0, 0], 2, down, right, send2, recv2),
+            send(sc.at[:, 1:7, 4], sc.at[:, 1:7, 0], 0, me_r, right, send2, recv2),
+            send(sc.at[:, 7, 4], sc.at[:, 7, 0], 1, me_r, right, send2, recv2),
+            send(sc.at[:, 8, 1:4], sc.at[:, 0, 1:4], 2, down, me_c, send2, recv2),
+            send(sc.at[:, 8, 4], sc.at[:, 0, 0], 3, down, right, send2, recv2),
         ]
 
     head_of = iota((1, 128), 1) >> 5
@@ -240,15 +244,17 @@
         d, a, b = BLOCK[n]
         return d, 2 * a + 1, 2 * b + 1
 
-    def block(first_n, mid_n, last_n, waits):
-        chains = [(64 * lo, 64 * hi) for lo, hi in ((first_n, mid_n), (mid_n, last_n))]
+    def block_attend(first_n, mid_n, last_n):
         for n in range(first_n, mid_n):
             _, i, j = spot_of(n)
-            g = jnp.concatenate([gc[i + u, j + v] for u in range(2) for v in range(2)], 0)
-            mask = dot_t(g, jnp.concatenate([g] * 4, 0)).astype(BF)
+            codes = jnp.concatenate([gc[i + u, j + v] for u in range(2) for v in range(2)], 0)
+            mask = dot_t(codes, jnp.concatenate([codes] * 4, 0)).astype(BF)
             for g in range(4):
                 for m in (n, n + mid_n - first_n):
                     attend(64 * m, 64, g, ones4[0, 0:256], mask)
+
+    def block_mlp(first_n, mid_n, last_n, waits):
+        chains = [(64 * lo, 64 * hi) for lo, hi in ((first_n, mid_n), (mid_n, last_n))]
         if waits:
             loads[1].wait()
         for lo, hi in chains:
@@ -285,70 +291,79 @@
             v = dot(att_s[128 * n : 128 * n + 128], cp[...])
             res = [jnp.concatenate(cells_of(sc, d, 2 * a, 2 * b), 0).astype(F32) for d in range(2)]
             past = res[0] + norm_rows(v[0:64])
-            ct_s[a, 64 * b : 64 * b + 64] = res[1] + norm_rows(v[64:128]) - past
-
+            ct_s[64 * n : 64 * n + 64] = res[1] + norm_rows(v[64:128]) - past
+
+    def difference(windows):
+        lo, hi = 64 * windows[0], 64 * windows[-1] + 64
+        operand = ct_s[lo:hi].astype(BF)
+        for n in range(4):
+            lanes = slice(256 * n, 256 * n + 256)
+            hid_s[lo:hi, lanes] = gelu_twice(dot(operand, du[:, lanes])).astype(BF)
+        v = dot(hid_s[lo:hi, 0:1024], dd[...])
+        for n in windows:
+            a, b = CROSS[n]
+            change = ct_s[64 * n : 64 * n + 64] + norm_rows(0.5 * v[64 * n - lo : 64 * n - lo + 64])
+            ch_s[a, 64 * b : 64 * b + 64] = change.astype(BF)
+
+    block_attend(*NEAR)
     if remote:
         @pl.when(early)
         def _():
-            block(*BLOCK_NEAR, True)
+            block_mlp(*NEAR, True)
             pl.semaphore_wait(barrier, 6)
             for copy in halo:
                 copy.start()
 
-        for copy in halo:
-            copy.wait_recv()
-    project(xc, far_block, wqkv)
-    unit(far_block, scale_s[0, 0:1])
+        halo[0].wait_recv()
+    project(xc, right_block, wqkv)
+    if remote:
+        halo[4].wait_recv()
+    unit(right_block, scale_s[0, 0:1])
+    block_attend(*RIGHT)
 
     @on(jnp.logical_not(early))
     def _():
         for n in range(1, 4):
             loads[n].wait()
 
-    block(*BLOCK_FAR, False)
-    if remote:
-        for copy in back:
+    block_mlp(*RIGHT, False)
+    if remote:
+        back[0].start()
+        for copy in halo[1:4] + halo[5:]:
+            copy.wait_recv()
+    project(xc, below_block, wqkv)
+    unit(below_block, scale_s[0, 0:1])
+    block_attend(*BELOW)
+    block_mlp(*BELOW, False)
+    if remote:
+        for copy in back[1:]:
             copy.start()
 
     @on(jnp.logical_not(early))
     def _():
-        block(*BLOCK_NEAR, False)
-
-    for n in range(4, 6):
+        block_mlp(*NEAR, False)
+
+    for n in range(4, 8):
         loads[n].wait()
     project(sc, own_cross, cqkv)
     unit(own_cross, scale_s[1, 0:1])
     cross(CROSS_NEAR)
+    difference(CROSS_NEAR)
     if remote:
         for copy in back:
             copy.wait_recv()
     project(sc, far_cross, cqkv)
     unit(far_cross, scale_s[1, 0:1])
     cross(CROSS_FAR)
-    for n in range(6, 8):
-        loads[n].wait()
+    difference(CROSS_FAR)
 
     oo = iota((128, 128), 0)
     tt = iota((128, 128), 1)
     r, c = oo >> 4, oo & 15
     spot = (c >> 3) * 64 + (r >> 2) * 32 + ((c >> 2) & 1) * 16 + (r & 3) * 4 + (c & 3)
     order = jnp.where(spot == tt, 1.0, 0.0).astype(BF)
-    halves = (0, 2)
-    for n in range(4):
-        lanes = slice(256 * n, 256 * n + 256)
-        for b in halves:
-            operand = ct_s[b : b + 2].reshape(256, C).astype(BF)
-            hid_s[128 * b : 128 * b + 256, lanes] = gelu_twice(dot(operand, du[:, lanes])).astype(BF)
-    for b in halves:
-        v = dot(hid_s[128 * b : 128 * b + 256, 0:1024], dd[...])
-        for n in range(2):
-            change = jnp.concatenate(
-                [
-                    (ct_s[b + n, p] + norm_rows(0.5 * v[128 * n + p.start : 128 * n + p.stop])).astype(BF)
-                    for p in pieces(128)
-                ], 0,
-            )
-            out[8 * (b + n) : 8 * (b + n) + 8] = dot(order, change).astype(BF).reshape(8, 16, C)
+    for band in range(4):
+        out[8 * band : 8 * band + 8] = dot(order, ch_s[band]).astype(BF).reshape(8, 16, C)
     if remote:
         for copy in halo + back:
             copy.wait_send()
@@ -380,9 +395,9 @@
             pltpu.VMEM((1024, C), BF),
             pltpu.VMEM((1024, 2048), BF),
             pltpu.VMEM((1024, C), BF),
-            pltpu.VMEM((4, 128, C), F32),
-            pltpu.VMEM((32, 16, C), BF),
-            dma, dma, dma((8,)), dma((2,)), dma((6,)), dma((6,)), dma((3,)), dma((3,)),
+            pltpu.VMEM((512, C), F32),
+            pltpu.VMEM((4, 128, C), BF),
+            dma, dma, dma((8,)), dma((7,)), dma((7,)), dma((4,)), dma((4,)),
         ],
         compiler_params=pltpu.CompilerParams(
             collective_id=0 if remote else None,

time: 38.7 us -> 36.6 us (0.946)
  Pallas kernels: 37.8 us -> 35.7 us
    pallas_call x1, Pallas kernels: 37.8 us -> 35.7 us  [device_program(): pl.pallas_call(functools.partial(kernel, rows, cols, remote), out_shape=p...]
where the time goes in v4:
time: 36.6 us; the launch traced here: 36.5 us
  Pallas kernels  35.7 us (98%)
  local copies, waits for them, and re-layouts  0.8 us (2%)
    pallas_call x1, Pallas kernels, device_program(): pl.pallas_call(functools.partial(kernel, rows, cols, remote), out_shape=p...  35.7 us
    unnamed x1, local copies, waits for them, and re-layouts  0.8 us

profile of v4, /device:TPU:6, one launch (start us, length us, event | category | flops | bytes accessed | tf_op | source)
XLA Modules:
  0.0 36.5 jit_solution(2450204877459017917)
XLA Ops:
  0.0 35.7 %window_pair.1 = bf16[32,16,512]{2,1,0:T(8,128)(2,1)S(1)} custom-call(bf16[2,32,16,512]{3,2,1,0:T(8,128)(2,1)} %img.1, s32[16,32]{1,0:T(8,128)} %bitcast.1, f32[16]{0:T(128)} %hs.1, f32[16]{0:T(128)} %cs.1, bf16[512,1536]{1,0:T(8,128)(2,1)} %wqkv_h.1, bf16[512,512]{1,0:T(8,128)(2,1)} %wp_h.1, bf16[512,2048]{1,0:T(8,128)(2,1)} %wu_h.1, ...), custom_call_target="tpu_custom_call" | custom-call | flops 11000000512 | bytes 13000000 | tf_op jit(solution)/shard_map/window_pair/pallas_call | solution.py:378
  35.7 0.8 %copy.14 = bf16[32,16,512]{2,1,0:T(8,128)(2,1)} copy(bf16[32,16,512]{2,1,0:T(8,128)(2,1)S(1)} %window_pair.1) | data formatting | bytes 1048576

commit v5 on v4

--- a/solution.py
+++ b/solution.py
@@ -34,13 +34,9 @@
 
 def norm_rows(v):
     mean = jnp.sum(v, axis=-1, keepdims=True) * (1.0 / C)
-    centre = v - mean
-    spread = jnp.sum(centre * centre, axis=-1, keepdims=True) * (1.0 / C)
-    return centre * lax.rsqrt(spread + EPS)
-
-
-def pieces(count, step=64):
-    return [slice(at, min(at + step, count)) for at in range(0, count, step)]
+    square = jnp.sum(v * v, axis=-1, keepdims=True) * (1.0 / C)
+    factor = lax.rsqrt(jnp.maximum(square - mean * mean, 0.0) + EPS)
+    return v * factor - mean * factor
 
 
 def gelu_twice(v):
@@ -54,7 +50,7 @@
 BLOCK += [(d, 3, b) for d in range(2) for b in range(2)]
 NEAR, RIGHT, BELOW = (0, 3, 6), (6, 9, 12), (12, 14, 16)
 CROSS = [(1, 1), (2, 1), (3, 1), (1, 0), (2, 0), (3, 0), (0, 0), (0, 1)]
-CROSS_NEAR, CROSS_FAR = range(3), range(3, 8)
+CROSS_NEAR, CROSS_MID, CROSS_FAR = range(3), range(3, 5), range(5, 8)
 
 
 def cell_rows():
@@ -76,7 +72,7 @@
     img, lab_h, hs, cs, wqkv_h, wp_h, wu_h, wd_h, cqkv_h, cp_h, du_h, dd_h,
     out,
     im, lab, wqkv, wp, wu, wd, cqkv, cp, du, dd,
-    xc, gc, sc, perm, bd, ones4, scale_s, qkv_s, att_s, hid_s, first_s, ct_s, ch_s,
+    xc, gc, sc, perm, bd, ones4, scale_s, qkv_s, cqkv_s, att_s, hid_s, first_s, ct_s, ch_s,
     im_sem, lab_sem, w_sem, send1, recv1, send2, recv2,
 ):
     me_r = lax.axis_index("row") if remote else 0
@@ -85,6 +81,7 @@
     left, right = lax.rem(me_c + cols - 1, cols), lax.rem(me_c + 1, cols)
 
     early = lax.rem(me_c, cols // 2) == 0
+    near_first = jnp.logical_or(early, lax.rem(me_c, 2) == 1)
 
     weights = [
         (wqkv_h, wqkv), (wp_h, wp), (wu_h, wu), (wd_h, wd),
@@ -124,25 +121,25 @@
 
     block_cells, cross_cells = cell_rows()
 
-    def project(ref, cells, w):
+    def project(held, ref, cells, w):
         for n in range(6):
             lanes = slice(256 * n, 256 * n + 256)
             for part in cells:
                 y = dot(jnp.concatenate([ref[spot] for spot, _ in part], 0), w[:, lanes]).astype(BF)
                 for m, (_, row) in enumerate(part):
-                    qkv_s[row : row + 16, lanes] = y[16 * m : 16 * m + 16]
-
-    def unit(cells, scale):
+                    held[row : row + 16, lanes] = y[16 * m : 16 * m + 16]
+
+    def unit(held, cells, scale):
         for n in range(4):
             lanes = slice(256 * n, 256 * n + 256)
             for part in cells:
-                y = jnp.concatenate([qkv_s[row : row + 16, lanes] for _, row in part], 0)
+                y = jnp.concatenate([held[row : row + 16, lanes] for _, row in part], 0)
                 factor = lax.rsqrt(jnp.maximum(dot(y * y, bd[...]), 1.0))
                 if n < 2:
                     factor = factor * scale[:, lanes]
-                y = (y.astype(F32) * factor).astype(BF)
+                y = y * factor.astype(BF)
                 for m, (_, row) in enumerate(part):
-                    qkv_s[row : row + 16, lanes] = y[16 * m : 16 * m + 16]
+                    held[row : row + 16, lanes] = y[16 * m : 16 * m + 16]
 
     def by_date(cells, here):
         return [[c for c in cells if c[0][0] == d and here(c[0]) ] for d in range(2)]
@@ -150,31 +147,34 @@
     own_block = by_date(block_cells, lambda c: c[1] < 8 and c[2] < 4)
     right_block = [[c for c in block_cells if c[0][1] < 7 and c[0][2] == 4]]
     below_block = [[c for c in block_cells if c[0][1] == 8 or c[0][1:] == (7, 4)]]
-    own_cross = by_date(cross_cells, lambda c: c[1] > 0 and c[2] > 0)
-    far_cross = by_date(cross_cells, lambda c: not (c[1] > 0 and c[2] > 0))
+    near_cross = by_date(cross_cells, lambda c: 0 < c[1] < 7 and 0 < c[2] < 3)
+    own_cross = [[c for c in cross_cells if min(c[0][1:]) > 0 and not (c[0][1] < 7 and c[0][2] < 3)]]
+    mid_cross = [[c for c in cross_cells if 1 < c[0][1] < 6 and c[0][2] == 0]]
+    far_cross = [[c for c in cross_cells if c[0][1] == 0 or (c[0][1] in (1, 6, 7) and c[0][2] == 0)]]
 
     def on(condition):
         return pl.when(condition) if remote else (lambda work: work())
 
     if remote:
         halo = [
-            send(xc.at[:, 1:7, 0], xc.at[:, 1:7, 4], 0, me_r, left, send1, recv1),
+            send(xc.at[0, 1:7, 0], xc.at[0, 1:7, 4], 0, me_r, left, send1, recv1),
             send(xc.at[:, 0, 1:4], xc.at[:, 8, 1:4], 1, up, me_c, send1, recv1),
             send(xc.at[:, 7, 0], xc.at[:, 7, 4], 2, me_r, left, send1, recv1),
             send(xc.at[:, 0, 0], xc.at[:, 8, 4], 3, up, left, send1, recv1),
             send(gc.at[1:8, 0], gc.at[1:8, 4], 4, me_r, left, send1, recv1),
             send(gc.at[0, 1:4], gc.at[8, 1:4], 5, up, me_c, send1, recv1),
             send(gc.at[0, 0], gc.at[8, 4], 6, up, left, send1, recv1),
+            send(xc.at[1, 1:7, 0], xc.at[1, 1:7, 4], 7, me_r, left, send1, recv1),
         ]
 
         @pl.when(jnp.logical_not(early))
         def _():
             pl.semaphore_wait(barrier, 6)
-            for copy in halo[:4]:
-                copy.start()
+            for n in (0, 7, 1, 2, 3):
+                halo[n].start()
 
     loads[0].wait()
-    project(xc, own_block, wqkv)
+    project(qkv_s, xc, own_block, wqkv)
     for load in loads[4:]:
         load.start()
 
@@ -190,7 +190,7 @@
             row = jnp.where(lane == h, ref[h] * LOG2E, row)
         scale_s[n] = row
 
-    unit(own_block, scale_s[0, 0:1])
+    unit(qkv_s, own_block, scale_s[0, 0:1])
 
     load_lab.wait()
     tok = iota((512, 16), 0)
@@ -210,7 +210,7 @@
     if remote:
         @pl.when(jnp.logical_not(early))
         def _():
-            for copy in halo[4:]:
+            for copy in halo[4:7]:
                 copy.start()
 
         back = [
@@ -226,11 +226,11 @@
     def stacked(v):
         return jnp.concatenate([v * head_mask[h] for h in range(4)], 0)
 
-    def attend(base, count, g, ones, mask):
+    def attend(held, base, count, g, ones, mask):
         lanes = slice(128 * g, 128 * g + 128)
-        q = qkv_s[base : base + count, lanes]
-        k = qkv_s[base : base + count, 512 + 128 * g : 640 + 128 * g]
-        v = qkv_s[base : base + count, 1024 + 128 * g : 1152 + 128 * g]
+        q = held[base : base + count, lanes]
+        k = held[base : base + count, 512 + 128 * g : 640 + 128 * g]
+        v = held[base : base + count, 1024 + 128 * g : 1152 + 128 * g]
         e = jnp.exp2(dot_t(q, stacked(k))).astype(BF)
         if mask is not None:
             e = e * mask
@@ -251,7 +251,7 @@
             mask = dot_t(codes, jnp.concatenate([codes] * 4, 0)).astype(BF)
             for g in range(4):
                 for m in (n, n + mid_n - first_n):
-                    attend(64 * m, 64, g, ones4[0, 0:256], mask)
+                    attend(qkv_s, 64 * m, 64, g, ones4[0, 0:256], mask)
 
     def block_mlp(first_n, mid_n, last_n, waits):
         chains = [(64 * lo, 64 * hi) for lo, hi in ((first_n, mid_n), (mid_n, last_n))]
@@ -285,7 +285,7 @@
     def cross(windows):
         for n in windows:
             for g in range(4):
-                attend(128 * n, 128, g, ones4[1], None)
+                attend(cqkv_s, 128 * n, 128, g, ones4[1], None)
         for n in windows:
             a, b = CROSS[n]
             v = dot(att_s[128 * n : 128 * n + 128], cp[...])
@@ -305,23 +305,34 @@
             change = ct_s[64 * n : 64 * n + 64] + norm_rows(0.5 * v[64 * n - lo : 64 * n - lo + 64])
             ch_s[a, 64 * b : 64 * b + 64] = change.astype(BF)
 
+    def near_windows(waits):
+        block_mlp(*NEAR, waits)
+        loads[4].wait()
+        project(cqkv_s, sc, near_cross, cqkv)
+        unit(cqkv_s, near_cross, scale_s[1, 0:1])
+
     block_attend(*NEAR)
     if remote:
         @pl.when(early)
         def _():
-            block_mlp(*NEAR, True)
             pl.semaphore_wait(barrier, 6)
-            for copy in halo:
-                copy.start()
-
+            for n in (0, 4, 7, 1, 2, 3, 5, 6):
+                halo[n].start()
+
+        @pl.when(near_first)
+        def _():
+            near_windows(True)
+
+    if remote:
         halo[0].wait_recv()
-    project(xc, right_block, wqkv)
+        halo[7].wait_recv()
+    project(qkv_s, xc, right_block, wqkv)
     if remote:
         halo[4].wait_recv()
-    unit(right_block, scale_s[0, 0:1])
+    unit(qkv_s, right_block, scale_s[0, 0:1])
     block_attend(*RIGHT)
 
-    @on(jnp.logical_not(early))
+    @on(jnp.logical_not(near_first))
     def _():
         for n in range(1, 4):
             loads[n].wait()
@@ -329,31 +340,36 @@
     block_mlp(*RIGHT, False)
     if remote:
         back[0].start()
-        for copy in halo[1:4] + halo[5:]:
+        for copy in halo[1:4] + halo[5:7]:
             copy.wait_recv()
-    project(xc, below_block, wqkv)
-    unit(below_block, scale_s[0, 0:1])
+    project(qkv_s, xc, below_block, wqkv)
+    unit(qkv_s, below_block, scale_s[0, 0:1])
     block_attend(*BELOW)
     block_mlp(*BELOW, False)
     if remote:
         for copy in back[1:]:
             copy.start()
 
-    @on(jnp.logical_not(early))
+    @on(jnp.logical_not(near_first))
     def _():
-        block_mlp(*NEAR, False)
-
-    for n in range(4, 8):
+        near_windows(False)
+
+    for n in range(5, 8):
         loads[n].wait()
-    project(sc, own_cross, cqkv)
-    unit(own_cross, scale_s[1, 0:1])
+    project(cqkv_s, sc, own_cross, cqkv)
+    unit(cqkv_s, own_cross, scale_s[1, 0:1])
     cross(CROSS_NEAR)
-    difference(CROSS_NEAR)
-    if remote:
-        for copy in back:
+    if remote:
+        back[0].wait_recv()
+    project(cqkv_s, sc, mid_cross, cqkv)
+    unit(cqkv_s, mid_cross, scale_s[1, 0:1])
+    cross(CROSS_MID)
+    difference(range(5))
+    if remote:
+        for copy in back[1:]:
             copy.wait_recv()
-    project(sc, far_cross, cqkv)
-    unit(far_cross, scale_s[1, 0:1])
+    project(cqkv_s, sc, far_cross, cqkv)
+    unit(cqkv_s, far_cross, scale_s[1, 0:1])
     cross(CROSS_FAR)
     difference(CROSS_FAR)
 
@@ -392,12 +408,13 @@
             pltpu.VMEM((2, 512, 128), BF),
             pltpu.VMEM((2, 8, C), F32),
             pltpu.VMEM((1024, 3 * C), BF),
+            pltpu.VMEM((1024, 3 * C), BF),
             pltpu.VMEM((1024, C), BF),
             pltpu.VMEM((1024, 2048), BF),
             pltpu.VMEM((1024, C), BF),
             pltpu.VMEM((512, C), F32),
             pltpu.VMEM((4, 128, C), BF),
-            dma, dma, dma((8,)), dma((7,)), dma((7,)), dma((4,)), dma((4,)),
+            dma, dma, dma((8,)), dma((8,)), dma((8,)), dma((4,)), dma((4,)),
         ],
         compiler_params=pltpu.CompilerParams(
             collective_id=0 if remote else None,

time: 36.6 us -> 34.2 us (0.934)
  the two profiles are of different devices: /device:TPU:6 before, /device:TPU:8 now
where the time goes in v5:
time: 34.2 us; the launch traced here: 34.1 us
  Pallas kernels  33.2 us (97%)
  local copies, waits for them, and re-layouts  0.8 us (2%)
    pallas_call x1, Pallas kernels, device_program(): pl.pallas_call(functools.partial(kernel, rows, cols, remote), out_shape=p...  33.2 us
    unnamed x1, local copies, waits for them, and re-layouts  0.8 us

profile of v5, /device:TPU:8, one launch (start us, length us, event | category | flops | bytes accessed | tf_op | source)
XLA Modules:
  0.0 34.1 jit_solution(17228914281881676033)
XLA Ops:
  0.0 33.2 %window_pair.1 = bf16[32,16,512]{2,1,0:T(8,128)(2,1)S(1)} custom-call(bf16[2,32,16,512]{3,2,1,0:T(8,128)(2,1)} %img.1, s32[16,32]{1,0:T(8,128)} %bitcast.1, f32[16]{0:T(128)} %hs.1, f32[16]{0:T(128)} %cs.1, bf16[512,1536]{1,0:T(8,128)(2,1)} %wqkv_h.1, bf16[512,512]{1,0:T(8,128)(2,1)} %wp_h.1, bf16[512,2048]{1,0:T(8,128)(2,1)} %wu_h.1, ...), custom_call_target="tpu_custom_call" | custom-call | flops 11000000512 | bytes 13000000 | tf_op jit(solution)/shard_map/window_pair/pallas_call | solution.py:394
  33.3 0.8 %copy.14 = bf16[32,16,512]{2,1,0:T(8,128)(2,1)} copy(bf16[32,16,512]{2,1,0:T(8,128)(2,1)S(1)} %window_pair.1) | data formatting | bytes 1048576

commit v6 on v5

--- a/solution.py
+++ b/solution.py
@@ -92,7 +92,6 @@
     load_im.start()
     load_lab = pltpu.make_async_copy(lab_h, lab, lab_sem)
     load_lab.start()
-    loads[0].start()
 
     if remote:
         barrier = pltpu.get_barrier_semaphore()
@@ -105,7 +104,7 @@
     perm[...] = jnp.where(src == t, 1.0, 0.0).astype(BF)
 
     load_im.wait()
-    for load in loads[1:4]:
+    for load in loads[0:4]:
         load.start()
     for d in range(2):
         for b in range(2):
@@ -172,25 +171,6 @@
             pl.semaphore_wait(barrier, 6)
             for n in (0, 7, 1, 2, 3):
                 halo[n].start()
-
-    loads[0].wait()
-    project(qkv_s, xc, own_block, wqkv)
-    for load in loads[4:]:
-        load.start()
-
-    bd[...] = jnp.where((o >> 5) == (t >> 5), 1.0, 0.0).astype(BF)
-    o4 = iota((512, 128), 0)
-    t4 = iota((512, 128), 1)
-    ones4[0] = jnp.where(((o4 >> 6) & 3) == (t4 >> 5), 1.0, 0.0).astype(BF)
-    ones4[1] = jnp.where((o4 >> 7) == (t4 >> 5), 1.0, 0.0).astype(BF)
-    lane = iota((8, C), 1) >> 5
-    for n, ref in ((0, hs), (1, cs)):
-        row = jnp.zeros((8, C), F32)
-        for h in range(HEADS):
-            row = jnp.where(lane == h, ref[h] * LOG2E, row)
-        scale_s[n] = row
-
-    unit(qkv_s, own_block, scale_s[0, 0:1])
 
     load_lab.wait()
     tok = iota((512, 16), 0)
@@ -213,6 +193,27 @@
             for copy in halo[4:7]:
                 copy.start()
 
+    loads[0].wait()
+    project(qkv_s, xc, own_block, wqkv)
+    for load in loads[4:]:
+        load.start()
+
+    bd[...] = jnp.where((o >> 5) == (t >> 5), 1.0, 0.0).astype(BF)
+    o4 = iota((512, 128), 0)
+    t4 = iota((512, 128), 1)
+    ones4[0] = jnp.where(((o4 >> 6) & 3) == (t4 >> 5), 1.0, 0.0).astype(BF)
+    ones4[1] = jnp.where((o4 >> 7) == (t4 >> 5), 1.0, 0.0).astype(BF)
+    lane = iota((8, C), 1) >> 5
+    for n, ref in ((0, hs), (1, cs)):
+        row = jnp.zeros((8, C), F32)
+        for h in range(HEADS):
+            row = jnp.where(lane == h, ref[h] * LOG2E, row)
+        scale_s[n] = row
+
+    unit(qkv_s, own_block, scale_s[0, 0:1])
+
+
+    if remote:
         back = [
             send(sc.at[:, 1:7, 4], sc.at[:, 1:7, 0], 0, me_r, right, send2, recv2),
             send(sc.at[:, 7, 4], sc.at[:, 7, 0], 1, me_r, right, send2, recv2),

time: 34.2 us -> 34.3 us (level)
  the two profiles are of different devices: /device:TPU:8 before, /device:TPU:1 now
where the time goes in v6:
time: 34.3 us; the launch traced here: 34.2 us
  Pallas kernels  33.4 us (97%)
  local copies, waits for them, and re-layouts  0.8 us (2%)
    pallas_call x1, Pallas kernels, device_program(): pl.pallas_call(functools.partial(kernel, rows, cols, remote), out_shape=p...  33.4 us
    unnamed x1, local copies, waits for them, and re-layouts  0.8 us

profile of v6, /device:TPU:1, one launch (start us, length us, event | category | flops | bytes accessed | tf_op | source)
XLA Modules:
  0.0 34.2 jit_solution(2364969559105434938)
XLA Ops:
  0.0 33.4 %window_pair.1 = bf16[32,16,512]{2,1,0:T(8,128)(2,1)S(1)} custom-call(bf16[2,32,16,512]{3,2,1,0:T(8,128)(2,1)} %img.1, s32[16,32]{1,0:T(8,128)} %bitcast.1, f32[16]{0:T(128)} %hs.1, f32[16]{0:T(128)} %cs.1, bf16[512,1536]{1,0:T(8,128)(2,1)} %wqkv_h.1, bf16[512,512]{1,0:T(8,128)(2,1)} %wp_h.1, bf16[512,2048]{1,0:T(8,128)(2,1)} %wu_h.1, ...), custom_call_target="tpu_custom_call" | custom-call | flops 11000000512 | bytes 13000000 | tf_op jit(solution)/shard_map/window_pair/pallas_call | solution.py:395
  33.4 0.8 %copy.14 = bf16[32,16,512]{2,1,0:T(8,128)(2,1)} copy(bf16[32,16,512]{2,1,0:T(8,128)(2,1)S(1)} %window_pair.1) | data formatting | bytes 1048576
